TPU v7x, 256 devices: a whole 4x4x8 slice. The times are simulated.
256 devices in a mesh: row: 32 (over z, x), col: 8 (over y, core).
Axes of the slice: x: 4, y: 4, z: 8, core: 2. Of those that a mesh axis runs over, the one named last changes fastest.
Arguments:
- x_dst: bfloat16 [32768, 256], P(('row', 'col')), may hold values from -96 to 96
- x_src: bfloat16 [8, 8192, 256], P('col', 'row'), may hold values from -96 to 96
- w_query: bfloat16 [256, 256], replicated, may hold values from -0.375 to 0.375
- w_key: bfloat16 [256, 256], replicated, may hold values from -0.375 to 0.375
- w_value: bfloat16 [256, 256], replicated, may hold values from -0.375 to 0.375
- w_out: bfloat16 [256, 256], replicated, may hold values from -1.5 to 1.5
- sink: float32 [8], replicated, may hold values from 2 to 8
- node_order: int32 [8, 8192], P('col'), may hold values from 0 to 8191, each once within a row
- tile_coords: int32 [32, 8, 2, 128], P('row', 'col'), may hold values from 0 to 63, as said below
- tile_count: int32 [32, 8], P('row', 'col'), may hold values from 32 to 128, as said below
- edge_mask: int32 [32, 8, 128, 128, 128], P('row', 'col'), may hold values 0 or 1
Outputs:
- attended: bfloat16 [32768, 256], P(('row', 'col'))
Inputs may be any that keep to these rules, and one draw needn't show every extreme that they name: tile_coords[r, c, 0, t] is a destination block below 8, tile_coords[r, c, 1, t] a source block below 64; the 128 pairs of one device are distinct. `tile_count`: some device uses all 128 slots in every draw. `node_order`: each row is a permutation.
All inputs are finite; a program needn't handle non-finite values. No bound on the sum of `edge_mask` on one device may be relied on, other than what follows from the above.
Results may differ from a plain program's by a relative error of at most 0.02195.
The roundings to bfloat16 on the way count: a program that leaves them out, or rounds other values in their place, can miss the bound.
Values may be sent and summed in bfloat16 or wider, within the bound.
A program may use at most 128 MiB of HBM per device.

v0:
```python
import math

import jax
import jax.numpy as jnp
from jax import lax
from jax.sharding import PartitionSpec as P

TILE_BLOCK = 8


def body(
    x_dst,
    x_src,
    w_query,
    w_key,
    w_value,
    w_out,
    sink,
    node_order,
    tile_coords,
    tile_count,
    edge_mask,
):
    heads = sink.shape[0]
    width = x_dst.shape[1]
    head_dim = width // heads
    tile = edge_mask.shape[-1]
    scale = 1.0 / math.sqrt(head_dim)
    query_own = jnp.dot(x_dst, w_query, preferred_element_type=jnp.float32).astype(jnp.bfloat16)
    queries = lax.all_gather(query_own, "col", axis=0, tiled=True)
    n_dblk = queries.shape[0] // tile
    query_blocks = queries.reshape(n_dblk, tile, width)
    w_both = jnp.concatenate([w_key, w_value], axis=1)
    own_pairs = jnp.dot(x_src[0], w_both, preferred_element_type=jnp.float32).astype(jnp.bfloat16)[
        None
    ]
    pairs = lax.all_gather(own_pairs, "row", axis=1, tiled=True)
    pairs = pairs[0][node_order[0]]
    n_sblk = pairs.shape[0] // tile
    pair_blocks = pairs.reshape(n_sblk, tile, 2 * width)
    coords = tile_coords[0, 0]
    count = tile_count[0, 0]
    masks = edge_mask[0, 0]
    n_steps = (count + TILE_BLOCK - 1) // TILE_BLOCK

    def block_scores(step):
        start = step * TILE_BLOCK
        rows = lax.dynamic_slice_in_dim(coords[0], start, TILE_BLOCK)
        cols = lax.dynamic_slice_in_dim(coords[1], start, TILE_BLOCK)
        live = start + jnp.arange(TILE_BLOCK, dtype=jnp.int32) < count
        edges = (lax.dynamic_slice_in_dim(masks, start, TILE_BLOCK, 0) == 1) & live[:, None, None]
        q_tiles = query_blocks[rows].reshape(TILE_BLOCK, tile, heads, head_dim)
        kv_tiles = pair_blocks[cols]
        k_tiles = kv_tiles[..., :width].reshape(TILE_BLOCK, tile, heads, head_dim)
        v_tiles = kv_tiles[..., width:].reshape(TILE_BLOCK, tile, heads, head_dim)
        scores = (
            jnp.einsum("tihd,tjhd->thij", q_tiles, k_tiles, preferred_element_type=jnp.float32)
            * scale
        )
        return (rows, edges[:, None], scores, v_tiles)

    acc_init = jnp.zeros((n_dblk, tile, width), jnp.float32)
    total_init = jnp.zeros((n_dblk, heads, tile), jnp.float32)

    def pass_max(step, maxima):
        rows, edges, scores, v_tiles = block_scores(step)
        rowmax = jnp.max(jnp.where(edges, scores, -1e30), axis=3)
        return maxima.at[rows].max(rowmax)

    local_max = lax.fori_loop(
        0, n_steps, pass_max, jnp.full((n_dblk, heads, tile), -1e30, jnp.float32)
    )
    maxima = lax.pmax(local_max.astype(jnp.bfloat16), "col").astype(local_max.dtype)
    top = jnp.maximum(maxima, sink[None, :, None])

    def pass_sum(step, carry):
        acc, total = carry
        rows, edges, scores, v_tiles = block_scores(step)
        weights = jnp.exp(jnp.where(edges, scores - top[rows][..., None], -1e30))
        total = total.at[rows].add(jnp.sum(weights, axis=3))
        mixed = jnp.einsum(
            "thij,tjhd->tihd",
            weights.astype(jnp.bfloat16),
            v_tiles,
            preferred_element_type=jnp.float32,
        )
        acc = acc.at[rows].add(mixed.reshape(TILE_BLOCK, tile, width))
        return (acc, total)

    acc, total = lax.fori_loop(0, n_steps, pass_sum, (acc_init, total_init))
    acc_own, total_own = (
        lax.psum_scatter(acc.astype(jnp.bfloat16), "col", scatter_dimension=0, tiled=True).astype(
            jnp.float32
        ),
        lax.psum_scatter(total.astype(jnp.bfloat16), "col", scatter_dimension=0, tiled=True).astype(
            jnp.float32
        ),
    )
    own_blocks = acc_own.shape[0]
    own_top = lax.dynamic_slice_in_dim(top, lax.axis_index("col") * own_blocks, own_blocks, 0)
    denom = total_own + jnp.exp(sink[None, :, None] - own_top)
    mixed = (
        acc_own.reshape(own_blocks, tile, heads, head_dim)
        / jnp.transpose(denom, (0, 2, 1))[..., None]
    )
    mixed = mixed.reshape(own_blocks * tile, width).astype(jnp.bfloat16)
    return jnp.dot(mixed, w_out, preferred_element_type=jnp.float32).astype(jnp.bfloat16)


def solution(mesh):
    in_specs = (
        P(("row", "col"), None),
        P("col", "row", None),
        P(),
        P(),
        P(),
        P(),
        P(),
        P("col", None),
        P("row", "col", None, None),
        P("row", "col"),
        P("row", "col", None, None, None),
    )
    out_specs = P(("row", "col"), None)
    return jax.shard_map(body, mesh=mesh, in_specs=in_specs, out_specs=out_specs, check_vma=False)
```

profile of v0, /device:TPU:4, one launch (start us, length us, event | category | flops | bytes accessed | tf_op | source)
XLA Modules:
  0.0 609.4 jit_solution(2928767303581218706)
XLA Ops:
  10.1 9.1 %copy.48 = s32[1,1,128,128,128]{3,4,2,1,0:T(8,128)} copy(s32[1,1,128,128,128]{4,3,2,1,0:T(8,128)} %param.25) | data formatting | bytes 16777216 | tf_op args[10]
  19.5 13.6 %all_gather.7 = bf16[1024,256]{1,0:T(8,128)(2,1)S(1)} all-gather(bf16[128,256]{1,0:T(8,128)(2,1)S(1)} %convolution_convert_fusion.2), channel_id=1, replica_groups=mesh['row'=32,'col'=8] {'col'}, dimensions={0}, use_global_device_ids=true | all-gather | bytes 589824 | tf_op jit(solution)/shard_map/all_gather | solution.py:30
  33.1 82.3 %all-gather.3.cloned.1.call-done = bf16[8192,512]{0,1:T(8,128)(2,1)} async-done(((bf16[256,512]{0,1:T(8,128)(2,1)}), bf16[8192,512]{0,1:T(8,128)(2,1)}) %all-gather.3.cloned.1.call-update) | async-done | bytes 8388624 | tf_op jit(solution)/shard_map/all_gather | solution.py:37
  115.4 11.9 %copy.47 = bf16[8192,512]{1,0:T(8,128)(2,1)} copy(bf16[8192,512]{0,1:T(8,128)(2,1)} %all-gather.3.cloned.1.call-done) | data formatting | bytes 16777216 | tf_op jit(solution)/shard_map/all_gather | solution.py:37
  127.4 38.2 %gather_fusion.5 = bf16[8192,512]{1,0:T(8,128)(2,1)} fusion(bf16[8192,512]{1,0:T(8,128)(2,1)} %copy.47, s32[8192]{0:T(1024)S(1)} %broadcast_clamp_fusion), kind=kCustom, calls=%fused_computation.5 | custom fusion | bytes 16809984 | tf_op jit(solution)/shard_map/gather | solution.py:38
  165.6 71.4 %while.22 = (s32[]{:T(128)}, f32[8,8,128]{2,1,0:T(8,128)S(1)}, s32[]{:T(128)}, s32[2,128]{1,0:T(2,128)S(1)}, s32[128,128,128]{1,2,0:T(8,128)}, /*index=5*/s32[]{...) while((s32[]{:T(128)}, f32[8,8,128]{2,1,0:T(8,128)S(1)}, ...), condition=%wide.region_3.4_spmd, body=%wide.region_0.3_spmd.sunk | while | flops 70518856 | bytes 8268267 | solution.py:70
  166.6 4.0 gather_fusion.1
  175.6 4.0 gather_fusion.1
  184.5 4.0 gather_fusion.1
  193.4 4.0 gather_fusion.1
  202.3 4.0 gather_fusion.1
  211.2 4.0 gather_fusion.1
  220.2 4.0 gather_fusion.1
  229.1 4.0 gather_fusion.1
  237.0 92.1 %pmax.7 = bf16[8,8,128]{2,1,0:T(8,128)(2,1)S(1)} all-reduce(bf16[8,8,128]{2,1,0:T(8,128)(2,1)S(1)} %convert_element_type.37), channel_id=1, replica_groups=mesh['row'=32,'col'=8] {'col'}, use_global_device_ids=true, to_apply=%region_4.5 | all-reduce | flops 8192 | bytes 32768 | tf_op jit(solution)/shard_map/pmax | solution.py:73
  330.3 117.9 %while.23 = (s32[]{:T(128)}, f32[8,128,256]{2,1,0:T(8,128)}, f32[8,8,128]{2,1,0:T(8,128)S(1)}, s32[]{:T(128)}, s32[2,128]{1,0:T(2,128)S(1)}, /*index=5*/bf16[64,...) while((s32[]{:T(128)}, f32[8,128,256]{2,1,0:T(8,128)}, ...), condition=%wide.region_9.10_spmd, body=%wide.region_5.9_spmd.sunk | while | flops 143132736 | bytes 25831996 | solution.py:90
  330.4 4.0 gather_fusion.2
  345.1 4.0 gather_fusion.2
  359.7 4.0 gather_fusion.2
  374.6 4.0 gather_fusion.2
  389.3 4.0 gather_fusion.2
  418.8 4.0 gather_fusion.2
  451.0 136.6 %all-reduce = bf16[8,8,128]{2,1,0:T(8,128)(2,1)S(1)} all-reduce(bf16[8,8,128]{2,1,0:T(8,128)(2,1)S(1)} %convert_element_type.40), channel_id=4, replica_groups=mesh['row'=32,'col'=8] {'col'}, use_global_device_ids=true, to_apply=%region_11.12.clone | all-reduce | flops 8192 | bytes 32768
  588.3 12.6 %reduce-scatter.2.cloned.1.call-done = bf16[1,128,256]{1,2,0:T(8,128)(2,1)} async-done(((bf16[8,128,256]{1,2,0:T(8,128)(2,1)}), bf16[1,128,256]{1,2,0:T(8,128)(2,1)}) %reduce-scatter.2.cloned.1.call-update) | async-done | bytes 65552 | tf_op jit(solution)/shard_map/reduce_scatter | solution.py:92
  (269 shorter events, 141.2 us)
Async XLA Ops:
  6.5 0.9 copy-start
  6.5 108.9 %all-gather.3.cloned.1.call-start = ((), (), s32[]{:S(2)}) async-start(), calls=%async_computation.2 | async-start | bytes 8650752 | tf_op jit(solution)/shard_map/all_gather | solution.py:37
  9.4 591.5 %reduce-scatter.2.cloned.1.call-start = ((), (), s32[]{:S(2)}) async-start(), calls=%async_computation.1 | async-start | bytes 589824 | tf_op jit(solution)/shard_map/reduce_scatter | solution.py:92
  10.1 9.1 %copy-start.5 = (s32[1,8192]{1,0:T(1,128)S(1)}, s32[1,8192]{1,0:T(1,128)}, u32[]{:S(2)}) copy-start(s32[1,8192]{1,0:T(1,128)} %param.22) | copy-start | bytes 98308
  10.1 9.1 %copy-start.1 = (bf16[256,256]{1,0:T(8,128)(2,1)S(1)}, bf16[256,256]{1,0:T(8,128)(2,1)}, u32[]{:S(2)}) copy-start(bf16[256,256]{1,0:T(8,128)(2,1)} %param.17) | copy-start | bytes 393220
  10.1 9.1 %copy-start.4 = (bf16[128,256]{1,0:T(8,128)(2,1)S(1)}, bf16[128,256]{1,0:T(8,128)(2,1)}, u32[]{:S(2)}) copy-start(bf16[128,256]{1,0:T(8,128)(2,1)} %param.15) | copy-start | bytes 196612
  127.4 38.3 %copy-start.3 = (s32[1,1,2,128]{3,2,1,0:T(2,128)S(1)}, s32[1,1,2,128]{3,2,1,0:T(2,128)}, u32[]{:S(2)}) copy-start(s32[1,1,2,128]{3,2,1,0:T(2,128)} %param.23) | copy-start | bytes 3076
  165.6 163.5 %copy-start.6 = (f32[8]{0:T(128)S(1)}, f32[8]{0:T(128)}, u32[]{:S(2)}) copy-start(f32[8]{0:T(128)} %param.21) | copy-start | bytes 100
  330.3 120.2 %copy-start.7 = (u32[256]{0:T(256)S(1)}, u32[256]{0:T(256)}, u32[]{:S(2)}) copy-start(u32[256]{0:T(256)} %constant.83) | copy-start | bytes 3076
  330.3 271.5 %copy-start.2 = (bf16[256,256]{1,0:T(8,128)(2,1)S(1)}, bf16[256,256]{1,0:T(8,128)(2,1)}, u32[]{:S(2)}) copy-start(bf16[256,256]{1,0:T(8,128)(2,1)} %param.20) | copy-start | bytes 393220
Sparse Core Ops, SparseCore 0:
  9.8 105.5 all-gather.2
  450.5 150.3 reduce-scatter.1
where the time goes:
time: 614 us; the launch traced here: 609 us
  blocking collectives  242 us (39%)
  local copies, waits for them, and re-layouts  157 us (26%)
  waiting for transfers between devices  95 us (15%)
  other arithmetic  71 us (12%)
  matrix products  28.7 us (5%)
  between operations  14.2 us (2%)
    unnamed x1, blocking collectives  137 us
    pmax x1, blocking collectives, body(): lax.pmax(local_max.astype(jnp.bfloat16), 'col').astype(local_max.dtype)  92.1 us
    all_gather x1, waiting for transfers between devices, body(): pairs = lax.all_gather(own_pairs, 'row', axis=1, tiled=True)  82.3 us
    gather x16, local copies, waits for them, and re-layouts, block_scores(): kv_tiles = pair_blocks[cols]  63.9 us
    gather x1, local copies, waits for them, and re-layouts, body(): pairs = pairs[0][node_order[0]]  38.2 us
    scatter-add x8, other arithmetic, pass_sum(): acc = acc.at[rows].add(mixed.reshape(TILE_BLOCK, tile, width))  26 us
    and x16, other arithmetic, block_scores(): (lax.dynamic_slice_in_dim(masks, start, TILE_BLOCK, 0) == 1) & live[:, No...  18.9 us
    dot_general x16, matrix products, block_scores(): jnp.einsum('tihd,tjhd->thij', q_tiles, k_tiles, preferred_element_type=jn...  18.3 us
  transfers between devices with their start and end apart: 2, of which 2 were waited for; matrix products, arithmetic and copies ran while one was open for 2% of the time, Pallas kernels for 0%

commit v1 on v0

v1 whole, which is shorter than its diff:
```python
import functools
import math

import jax
import jax.numpy as jnp
from jax import lax
from jax.experimental import pallas as pl
from jax.experimental.pallas import tpu as pltpu
from jax.sharding import PartitionSpec as P

MASKED = -1e30
UNROLL = 8
TILE = 128


def dot_nt(a, b):
    return lax.dot_general(a, b, (((1,), (1,)), ((), ())), preferred_element_type=jnp.float32)


def attend_kernel(
    order_ref, coords_ref, count_ref, sink_ref, x_ref, q_ref, wk_ref, wvt_ref, bias_hbm,
    acc_out, stat_out,
    rows, lo, hi, keys, values, qz, acc, top, total, bias, sbuf, peak, sem,
):
    heads = sink_ref.shape[0]
    n_dblk, width, tile = q_ref.shape
    hd = width // heads
    half = width // 2
    per_half = heads // 2
    c = math.log2(math.e) / math.sqrt(hd)
    nsrc = x_ref.shape[0]
    nblk = nsrc // tile
    slots = bias_hbm.shape[0]
    count = count_ref[0]
    load = pltpu.make_async_copy(bias_hbm, bias.at[pl.ds(0, slots)], sem.at[0])
    load.start()

    @pl.loop(0, nsrc // 256)
    def _(i):
        r = pl.ds(pl.multiple_of(i * 256, 256), 256)
        v = x_ref[r, :].astype(jnp.float32)
        rows[0, r, :] = v[:, :half]
        rows[1, r, :] = v[:, half:]

    qz[...] = jnp.zeros_like(qz)
    for d in range(n_dblk):
        for h in range(heads):
            hh = h % per_half
            qz[d, hh * hd:(hh + 1) * hd, h * tile:(h + 1) * tile] = q_ref[d, h * hd:(h + 1) * hd, :]

    bias[slots] = jnp.full(bias.shape[1:], MASKED, jnp.bfloat16)
    acc[...] = jnp.zeros_like(acc)
    total[...] = jnp.zeros_like(total)
    for d in range(n_dblk):
        for h in range(heads):
            top[d, h:h + 1, :] = jnp.full((1, tile), sink_ref[h] * math.sqrt(hd), jnp.float32)

    wk = wk_ref[...]
    wvt = wvt_ref[...]

    def gather(b, e):
        base = b * tile
        for r in range(tile):
            idx = order_ref[base + r]
            lo[e, r:r + 1, :] = rows[0, pl.ds(idx, 1), :]
            hi[e, r:r + 1, :] = rows[1, pl.ds(idx, 1), :]

    def project(b, e):
        x = jnp.concatenate([lo[e].astype(jnp.bfloat16), hi[e].astype(jnp.bfloat16)], axis=1)
        keys[b] = jnp.dot(x, wk, preferred_element_type=jnp.float32).astype(jnp.bfloat16)
        values[b] = dot_nt(wvt, x).astype(jnp.bfloat16)

    gather(0, 0)

    @pl.loop(0, nblk // 2)
    def _(i):
        gather(2 * i + 1, 1)
        project(2 * i, 0)
        gather(jnp.minimum(2 * i + 2, nblk - 1), 0)
        project(2 * i + 1, 1)

    load.wait()
    ones = jnp.ones((16, tile), jnp.bfloat16)

    def place(t):
        u = jnp.minimum(t, slots - 1)
        return coords_ref[0, u], coords_ref[1, u]

    def scores(t, e):
        d, b = place(t)
        bt = bias[jnp.where(t < count, t, slots)].astype(jnp.float32)
        for hp in range(heads // 2):
            g = 2 * hp // per_half
            pair = jnp.dot(
                keys[b, :, g * half:(g + 1) * half],
                qz[d, :, 2 * hp * tile:2 * (hp + 1) * tile],
                preferred_element_type=jnp.float32,
            )
            for i in range(2):
                s = pair[:, i * tile:(i + 1) * tile] + bt
                sbuf[e, 2 * hp + i] = s
                peak[e, 2 * hp + i:2 * hp + i + 1, :] = jnp.max(s, axis=0, keepdims=True)

    def weigh(t, e):
        d, b = place(t)
        before = top[d]
        now = jnp.maximum(before, peak[e])
        fade = jnp.exp2((before - now) * c)
        top[d] = now
        sums = []
        for h in range(heads):
            f = slice(h * hd, (h + 1) * hd)
            p = jnp.exp2((sbuf[e, h] - now[h:h + 1]) * c).astype(jnp.bfloat16)
            v = jnp.concatenate([values[b, f, :], ones], axis=0)
            o = jnp.dot(v, p, preferred_element_type=jnp.float32)
            acc[d, f, :] = acc[d, f, :] * fade[h:h + 1] + o[:hd]
            sums.append(o[hd:hd + 1])
        total[d] = total[d] * fade + jnp.concatenate(sums, axis=0)

    scores(0, 0)

    @pl.loop(0, (count + UNROLL - 1) // UNROLL)
    def _(i):
        for u in range(UNROLL):
            t = i * UNROLL + u
            scores(t + 1, (u + 1) % 2)
            weigh(t, u % 2)

    acc_out[...] = acc[...].astype(jnp.bfloat16)
    for d in range(n_dblk):
        stat_out[d, :heads, :] = top[d] * c
        stat_out[d, heads:, :] = total[d]


def attend(order, coords, count, sink, x, q, wk, wvt, bias):
    nsrc, width = x.shape
    n_dblk, _, tile = q.shape
    heads = sink.shape[0]
    slots = bias.shape[0]
    nblk = nsrc // tile
    smem = pl.BlockSpec(memory_space=pltpu.SMEM)
    vmem = pl.BlockSpec(memory_space=pltpu.VMEM)
    return pl.pallas_call(
        attend_kernel,
        out_shape=(
            jax.ShapeDtypeStruct((n_dblk, width, tile), jnp.bfloat16),
            jax.ShapeDtypeStruct((n_dblk, 2 * heads, tile), jnp.float32),
        ),
        in_specs=[smem] * 4 + [vmem] * 4 + [pl.BlockSpec(memory_space=pl.ANY)],
        out_specs=(vmem, vmem),
        scratch_shapes=[
            pltpu.VMEM((2, nsrc, width // 2), jnp.float32),
            pltpu.VMEM((2, tile, width // 2), jnp.float32),
            pltpu.VMEM((2, tile, width // 2), jnp.float32),
            pltpu.VMEM((nblk, tile, width), jnp.bfloat16),
            pltpu.VMEM((nblk, width, tile), jnp.bfloat16),
            pltpu.VMEM((n_dblk, width // 2, heads * tile), jnp.bfloat16),
            pltpu.VMEM((n_dblk, width, tile), jnp.float32),
            pltpu.VMEM((n_dblk, heads, tile), jnp.float32),
            pltpu.VMEM((n_dblk, heads, tile), jnp.float32),
            pltpu.VMEM((slots + 1, tile, tile), jnp.bfloat16),
            pltpu.VMEM((2, heads, tile, tile), jnp.float32),
            pltpu.VMEM((2, heads, tile), jnp.float32),
            pltpu.SemaphoreType.DMA((1,)),
        ],
        compiler_params=pltpu.CompilerParams(vmem_limit_bytes=56 * 2**20),
        name="attend",
    )(order, coords, count, sink, x, q, wk, wvt, bias)


def body(
    x_dst, x_src, w_query, w_key, w_value, w_out, sink, node_order, tile_coords, tile_count, edge_mask
):
    heads = sink.shape[0]
    width = x_dst.shape[1]
    hd = width // heads
    tile = edge_mask.shape[-1]
    x = lax.all_gather(x_src[0], "row", axis=0, tiled=True)
    q_own = dot_nt(w_query.T, x_dst).astype(jnp.bfloat16)
    q = lax.all_gather(q_own, "col", axis=0)
    bias = jnp.where(edge_mask[0, 0] == 1, 0.0, MASKED).astype(jnp.bfloat16).swapaxes(1, 2)
    acc, stat = attend(
        node_order[0], tile_coords[0, 0], tile_count[0], sink, x, q, w_key, w_value.T, bias
    )
    acc = lax.all_to_all(acc, "col", 0, 0).astype(jnp.float32)
    stat = lax.all_to_all(stat, "col", 0, 0)
    tops, totals = stat[:, :heads], stat[:, heads:]
    top = jnp.max(tops, axis=0)
    fade = jnp.exp2(tops - top)
    denom = jnp.sum(totals * fade, axis=0) + jnp.exp2(sink[:, None] * math.log2(math.e) - top)
    acc = jnp.sum(acc.reshape(-1, heads, hd, tile) * fade[:, :, None, :], axis=0)
    mixed = (acc / denom[:, None, :]).reshape(width, tile).T.astype(jnp.bfloat16)
    return jnp.dot(mixed, w_out, preferred_element_type=jnp.float32).astype(jnp.bfloat16)


def solution(mesh):
    in_specs = (
        P(("row", "col"), None),
        P("col", "row", None),
        P(),
        P(),
        P(),
        P(),
        P(),
        P("col", None),
        P("row", "col", None, None),
        P("row", "col"),
        P("row", "col", None, None, None),
    )
    out_specs = P(("row", "col"), None)
    return jax.shard_map(body, mesh=mesh, in_specs=in_specs, out_specs=out_specs, check_vma=False)
```

time: 614 us -> 170 us (0.28)
  blocking collectives: 242 us -> 14.7 us
  local copies, waits for them, and re-layouts: 157 us -> 9.82 us
  other arithmetic: 71 us -> 6.94 us
  Pallas kernels: 0 us -> 43.3 us
  matrix products: 28.7 us -> 1.05 us
  waiting for transfers between devices: 95 us -> 70.1 us
  starting transfers between devices: 0.04 us -> 6.86 us
    unnamed x1 -> x0, blocking collectives: 137 us -> none
    gather x57 -> x0, local copies, waits for them, and re-layouts: 120 us -> none  [the longest x16 63.9 us: block_scores(): kv_tiles = pair_blocks[cols]]
    pmax x1 -> x0, blocking collectives: 92.1 us -> none  [body(): lax.pmax(local_max.astype(jnp.bfloat16), 'col').astype(local_max.dtype)]
    pallas_call x0 -> x1, Pallas kernels: none -> 43.3 us  [attend(): pl.pallas_call(attend_kernel, out_shape=(jax.ShapeDtypeStruct((n_dblk, wi...]
    scatter-add x16 -> x0, other arithmetic: 32.2 us -> none  [the longest x8 26 us: pass_sum(): acc = acc.at[rows].add(mixed.reshape(TILE_BLOCK, tile, width))]
    all_gather x1, waiting for transfers between devices: 82.3 us -> 53.8 us  [body(): x = lax.all_gather(x_src[0], 'row', axis=0, tiled=True)]
    dot_general x26 -> x1, matrix products: 27.9 us -> 0.22 us  [dot_nt(): lax.dot_general(a, b, (((1,), (1,)), ((), ())), preferred_element_type=jn...]
    and x16 -> x0, other arithmetic: 18.9 us -> none  [block_scores(): (lax.dynamic_slice_in_dim(masks, start, TILE_BLOCK, 0) == 1) & live[:, No...]
  transfers between devices with their start and end apart: 2 -> 3, of which waited for: 2 -> 3; matrix products, arithmetic and copies ran while one was open for 2% -> 10% of each run, Pallas kernels for 0% -> 0%
where the time goes in v1:
time: 170 us; the launch traced here: 167 us
  waiting for transfers between devices  70.1 us (41%)
  Pallas kernels  43.3 us (25%)
  blocking collectives  14.7 us (9%)
  between operations  14.2 us (8%)
  local copies, waits for them, and re-layouts  9.82 us (6%)
  other arithmetic  6.94 us (4%)
  starting transfers between devices  6.86 us (4%)
    all_gather x1, waiting for transfers between devices, body(): x = lax.all_gather(x_src[0], 'row', axis=0, tiled=True)  53.8 us
    pallas_call x1, Pallas kernels, attend(): pl.pallas_call(attend_kernel, out_shape=(jax.ShapeDtypeStruct((n_dblk, wi...  43.3 us
    all_gather x1, blocking collectives, body(): q = lax.all_gather(q_own, 'col', axis=0)  14.7 us
    all_to_all x1, waiting for transfers between devices, body(): acc = lax.all_to_all(acc, 'col', 0, 0).astype(jnp.float32)  10.1 us
    unnamed x12, local copies, waits for them, and re-layouts  9.82 us
    transpose x1, other arithmetic, body(): jnp.where(edge_mask[0, 0] == 1, 0.0, MASKED).astype(jnp.bfloat16)  6.7 us
    all_to_all x1, waiting for transfers between devices, body(): stat = lax.all_to_all(stat, 'col', 0, 0)  5.52 us
    all_to_all x1, starting transfers between devices, body(): acc = lax.all_to_all(acc, 'col', 0, 0).astype(jnp.float32)  3.49 us
  transfers between devices with their start and end apart: 3, of which 3 were waited for; matrix products, arithmetic and copies ran while one was open for 10% of the time, Pallas kernels for 0%

profile of v1, /device:TPU:4, one launch (start us, length us, event | category | flops | bytes accessed | tf_op | source)
XLA Modules:
  0.0 167.0 jit_solution(2324578869261899994)
XLA Ops:
  6.5 0.0 copy-start
  6.5 0.0 all-gather.4.cloned.1.call-start
  6.5 0.7 all-gather.4.cloned.1.call-update
  7.3 0.0 copy-start.1
  7.3 0.0 copy-start.3
  7.3 9.1 %copy.13 = s32[1,1,128,128,128]{3,4,2,1,0:T(8,128)} copy(s32[1,1,128,128,128]{4,3,2,1,0:T(8,128)} %param.21) | data formatting | bytes 16777216 | tf_op args[10]
  16.3 0.0 copy-done.1
  16.3 0.7 copy.12
  17.7 0.0 copy-done
  17.7 0.0 copy-done.3
  17.8 0.2 convolution_convert_fusion.1
  18.0 14.7 %all-gather.1 = bf16[2048,128]{1,0:T(8,128)(2,1)} all-gather(bf16[256,128]{1,0:T(8,128)(2,1)S(1)} %convolution_convert_fusion.1), channel_id=3, replica_groups=mesh['row'=32,'col'=8] {'col'}, dimensions={0}, use_global_device_ids=true | all-gather | bytes 589824 | tf_op jit(solution)/shard_map/all_gather | solution.py:180
  32.7 6.7 %fusion.bias_hbm = bf16[128,128,128]{2,1,0:T(8,128)(2,1)} fusion(s32[1,1,128,128,128]{3,4,2,1,0:T(8,128)} %copy.13), kind=kLoop, calls=%fused_computation.1 | loop fusion | flops 6291456 | bytes 12582912 | tf_op jit(solution)/shard_map/transpose | solution.py:181
  39.4 53.8 %all-gather.4.cloned.1.call-done = bf16[1,8192,256]{2,1,0:T(8,128)(2,1)} async-done(((bf16[1,256,256]{2,1,0:T(8,128)(2,1)}), bf16[1,8192,256]{2,1,0:T(8,128)(2,1)}) %all-gather.4.cloned.1.call-update) | async-done | bytes 4194320 | tf_op jit(solution)/shard_map/all_gather | solution.py:178
  93.1 43.3 %attend.1 = (bf16[8,256,128]{2,1,0:T(8,128)(2,1)}, f32[8,16,128]{2,1,0:T(8,128)}) custom-call(s32[8192]{0:T(1024)} %bitcast.26, s32[2,128]{1,0:T(2,128)} %bitcast.27, s32[1]{0:T(128)} %bitcast.22.count_ref, f32[8]{0:T(128)} %sink_ref.1, bf16[8192,256]{1,0:T(8,128)(2,1)} %bitcast.23, bf16[8,256,128]{2,1,0:T(8,128)(2,1)} %bitcast.24, bf16[256,256]{1,0:T(8,128)(2,1)} %wk_ref.1, ...), custom_call_target="tpu_custom_call" | custom-call | tf_op jit(solution)/shard_map/attend/pallas_call | solution.py:143
  136.5 3.4 %all-to-all-start.1 = ((f32[8,16,128]{2,1,0:T(8,128)}), f32[8,16,128]{2,1,0:T(8,128)S(1)}, u32[]{:S(2)}, u32[]{:S(2)}) async-start(f32[8,16,128]{2,1,0:T(8,128)} %get-tuple-element.8), calls=%async_computation.1 | async-start | bytes 131072 | tf_op jit(solution)/shard_map/all_to_all | solution.py:186
  139.9 0.0 copy-done.4
  139.9 5.5 %all-to-all-done.1 = f32[8,16,128]{2,1,0:T(8,128)S(1)} async-done(((f32[8,16,128]{2,1,0:T(8,128)}), f32[8,16,128]{2,1,0:T(8,128)S(1)}, u32[]{:S(2)}, u32[]{:S(2)}) %all-to-all-start.1) | async-done | bytes 65568 | tf_op jit(solution)/shard_map/all_to_all | solution.py:186
  145.4 3.5 %all-to-all-start = ((bf16[8,256,128]{2,1,0:T(8,128)(2,1)}), bf16[8,256,128]{2,1,0:T(8,128)(2,1)S(1)}, u32[]{:S(2)}, u32[]{:S(2)}) async-start(bf16[8,256,128]{2,1,0:T(8,128)(2,1)} %get-tuple-element.7), calls=%async_computation | async-start | bytes 1048576 | tf_op jit(solution)/shard_map/all_to_all | solution.py:185
  148.9 0.1 exponential_add_fusion
  149.0 10.1 %all-to-all-done = bf16[8,256,128]{2,1,0:T(8,128)(2,1)S(1)} async-done(((bf16[8,256,128]{2,1,0:T(8,128)(2,1)}), bf16[8,256,128]{2,1,0:T(8,128)(2,1)S(1)}, u32[]{:S(2)}, u32[]{:S(2)}) %all-to-all-start) | async-done | bytes 524320 | tf_op jit(solution)/shard_map/all_to_all | solution.py:185
  159.2 0.1 fusion.1
  159.3 0.0 copy-done.2
  159.3 0.8 convolution_convert_fusion
  (6 shorter events, 0.1 us)
Async XLA Ops:
  6.5 11.2 %copy-start = (bf16[256,256]{1,0:T(8,128)(2,1)S(1)}, bf16[256,256]{1,0:T(8,128)(2,1)}, u32[]{:S(2)}) copy-start(bf16[256,256]{1,0:T(8,128)(2,1)} %param.13) | copy-start | bytes 393220
  6.5 86.6 %all-gather.4.cloned.1.call-start = ((), (), s32[]{:S(2)}) async-start(), calls=%async_computation.2 | async-start | bytes 4325376 | tf_op jit(solution)/shard_map/all_gather | solution.py:178
  7.3 9.1 %copy-start.1 = (bf16[256,256]{1,0:T(8,128)(2,1)S(1)}, bf16[256,256]{1,0:T(8,128)(2,1)}, u32[]{:S(2)}) copy-start(bf16[256,256]{1,0:T(8,128)(2,1)} %param.15) | copy-start | bytes 393220
  7.3 10.5 %copy-start.3 = (bf16[128,256]{1,0:T(8,128)(2,1)S(1)}, bf16[128,256]{1,0:T(8,128)(2,1)}, u32[]{:S(2)}) copy-start(bf16[128,256]{1,0:T(8,128)(2,1)} %param.11) | copy-start | bytes 196612
  32.7 107.2 %copy-start.4 = (f32[8]{0:T(128)S(1)}, f32[8]{0:T(128)}, u32[]{:S(2)}) copy-start(f32[8]{0:T(128)} %sink_ref.1) | copy-start | bytes 100
  39.4 119.9 %copy-start.2 = (bf16[256,256]{1,0:T(8,128)(2,1)S(1)}, bf16[256,256]{1,0:T(8,128)(2,1)}, u32[]{:S(2)}) copy-start(bf16[256,256]{1,0:T(8,128)(2,1)} %param.16) | copy-start | bytes 393220
  136.5 8.9 %all-to-all-start.1 = ((f32[8,16,128]{2,1,0:T(8,128)}), f32[8,16,128]{2,1,0:T(8,128)S(1)}, u32[]{:S(2)}, u32[]{:S(2)}) async-start(f32[8,16,128]{2,1,0:T(8,128)} %get-tuple-element.8), calls=%async_computation.1 | async-start | bytes 131072 | tf_op jit(solution)/shard_map/all_to_all | solution.py:186
  145.4 13.8 %all-to-all-start = ((bf16[8,256,128]{2,1,0:T(8,128)(2,1)}), bf16[8,256,128]{2,1,0:T(8,128)(2,1)S(1)}, u32[]{:S(2)}, u32[]{:S(2)}) async-start(bf16[8,256,128]{2,1,0:T(8,128)(2,1)} %get-tuple-element.7), calls=%async_computation | async-start | bytes 1048576 | tf_op jit(solution)/shard_map/all_to_all | solution.py:185
Sparse Core Ops, SparseCore 0:
  9.9 83.1 all-gather.3

commit v2 on v1

--- a/solution.py
+++ b/solution.py
@@ -17,8 +17,200 @@
     return lax.dot_general(a, b, (((1,), (1,)), ((), ())), preferred_element_type=jnp.float32)
 
 
+MESH = pl.DeviceIdType.MESH
+LINKS = ("x+", "x-", "z+", "z-")
+STEP = {"x+": (1, 0), "x-": (-1, 0), "z+": (0, 1), "z-": (0, -1)}
+SPLIT = 96
+
+
+def spread_plan(nx, nz, rows):
+    cut = {"A": (0, SPLIT // 2, SPLIT), "B": (SPLIT, (SPLIT + rows) // 2, rows)}
+    sends, events, free, pending = [], [], {link: 0.0 for link in LINKS}, []
+
+    def issue(now, kind, link, ox, oz, lo, hi):
+        if hi <= lo:
+            return
+        start = max(free[link], now)
+        free[link] = start + (hi - lo)
+        pending.append((free[link] + 60.0, len(sends), kind))
+        sends.append((link, ox, oz, lo, hi - lo))
+        events.append(("send", len(sends) - 1))
+
+    def clip(kind, link, k, half, lo, hi):
+        if k + 1 < half:
+            return lo, hi
+        if k + 1 > half:
+            return lo, lo
+        a, m, b = cut[kind]
+        return (max(lo, a), min(hi, m)) if link[1] == "+" else (max(lo, m), min(hi, b))
+
+    for kind, order in (("B", ("z+", "z-")), ("A", ("x+", "x-")), ("A", ("z+", "z-")), ("B", ("x+", "x-"))):
+        for link in order:
+            issue(0.0, kind, link, 0, 0, cut[kind][0], cut[kind][2])
+    while pending:
+        pending.sort()
+        now, k, kind = pending.pop(0)
+        link, ox, oz, lo, n = sends[k]
+        hi = lo + n
+        events.append(("recv", k))
+        ox, oz = ox - STEP[link][0], oz - STEP[link][1]
+        on_x = link[0] == "x"
+        first = on_x == (kind == "A")
+        far, half = (abs(ox), nx // 2) if on_x else (abs(oz), nz // 2)
+        a, b = clip(kind, link, far, half, lo, hi)
+        issue(now, kind, link, ox, oz, a, b)
+        if first:
+            for other in ("z+", "z-") if on_x else ("x+", "x-"):
+                a, b = clip(kind, other, 0, nz // 2 if on_x else nx // 2, lo, hi)
+                issue(now, kind, other, ox, oz, a, b)
+    return sends, events
+
+
+def gather_kernel(
+    nx, nz, ncol, sends, events,
+    x_dst, w_query, x_src, mask_hbm,
+    x_all, q_all, bias_hbm,
+    q_own, masks, bias, send_sem, recv_sem, q_send, q_recv, in_sem, out_sem, own_sem,
+):
+    row, col = lax.axis_index("row"), lax.axis_index("col")
+    z, x = row // nx, lax.rem(row, nx)
+    slots = masks.shape[0]
+    chunks = in_sem.shape[0]
+    per = slots // chunks
+
+    def loaded(i):
+        part = pl.ds(i * per, per)
+        return pltpu.make_async_copy(mask_hbm.at[part], masks.at[part], in_sem.at[i])
+
+    def stored(i):
+        part = pl.ds(i * per, per)
+        return pltpu.make_async_copy(bias.at[part], bias_hbm.at[part], out_sem.at[i])
+
+    def at(ox, oz):
+        return lax.rem(z + oz + nz, nz) * nx + lax.rem(x + ox + nx, nx)
+
+    def peer(o):
+        return lax.rem(col + o, ncol)
+
+    barrier = pltpu.get_barrier_semaphore()
+    for link in LINKS:
+        pl.semaphore_signal(barrier, inc=1, device_id={"row": at(*STEP[link])}, device_id_type=MESH)
+    for o in range(1, ncol):
+        pl.semaphore_signal(barrier, inc=1, device_id={"col": peer(o)}, device_id_type=MESH)
+    for i in range(chunks):
+        loaded(i).start()
+    own_x = pltpu.make_async_copy(x_src, x_all.at[row], own_sem.at[0])
+    own_x.start()
+    pl.semaphore_wait(barrier, len(LINKS) + ncol - 1)
+
+    def piece(k, arriving):
+        link, ox, oz, lo, n = sends[k]
+        dx, dz = STEP[link]
+        origin = at(ox - dx, oz - dz) if arriving else at(ox, oz)
+        part = pl.ds(lo, n)
+        own = ox == 0 and oz == 0 and not arriving
+        return pltpu.make_async_remote_copy(
+            src_ref=x_src.at[part] if own else x_all.at[origin, part],
+            dst_ref=x_all.at[origin, part],
+            send_sem=send_sem.at[k],
+            recv_sem=recv_sem.at[k],
+            device_id={"row": at(dx, dz)},
+            device_id_type=MESH,
+        )
+
+    def query(o, slot):
+        return pltpu.make_async_remote_copy(
+            src_ref=q_own,
+            dst_ref=q_all.at[slot],
+            send_sem=q_send.at[o - 1],
+            recv_sem=q_recv.at[o - 1],
+            device_id={"col": peer(o)},
+            device_id_type=MESH,
+        )
+
+    share = -(-slots // (len(sends) - 8))
+
+    def turn(first, last):
+        @pl.loop(first, last)
+        def _(t):
+            bias[t] = jnp.where(masks[t] == 1, 0.0, MASKED).T.astype(jnp.bfloat16)
+
+    def work(first, last):
+        for i in range(chunks):
+            if first <= i * per < last:
+                loaded(i).wait()
+        turn(first, last)
+        for i in range(chunks):
+            if first < (i + 1) * per <= last:
+                stored(i).start()
+
+    own_q = None
+    done = 0
+    for n, (what, k) in enumerate(events):
+        if what == "send":
+            piece(k, False).start()
+        else:
+            if own_q is None:
+                q = jnp.dot(x_dst[...], w_query[...], preferred_element_type=jnp.float32)
+                q_own[...] = q.T.astype(jnp.bfloat16)
+                for o in range(1, ncol):
+                    query(o, col).start()
+                own_q = pltpu.make_async_copy(q_own, q_all.at[col], own_sem.at[1])
+                own_q.start()
+            piece(k, True).wait_recv()
+        if own_q is not None and done < slots and events[n + 1][0] == "recv":
+            end = min(slots, done + share)
+            work(done, end)
+            done = end
+    for o in range(1, ncol):
+        query(o, lax.rem(col - o + ncol, ncol)).wait_recv()
+    for k in range(len(sends)):
+        piece(k, False).wait_send()
+    for o in range(1, ncol):
+        query(o, col).wait_send()
+    for i in range(chunks):
+        stored(i).wait()
+    own_x.wait()
+    own_q.wait()
+
+
+def gather_all(nx, nz, ncol, x_dst, w_query, x_src, mask):
+    rows, width = x_src.shape
+    slots, tile, _ = mask.shape
+    sends, events = spread_plan(nx, nz, rows)
+    vmem = pl.BlockSpec(memory_space=pltpu.VMEM)
+    hbm = pl.BlockSpec(memory_space=pl.ANY)
+    dma = pltpu.SemaphoreType.DMA
+    return pl.pallas_call(
+        functools.partial(gather_kernel, nx, nz, ncol, sends, events),
+        out_shape=(
+            jax.ShapeDtypeStruct((nx * nz, rows, width), jnp.bfloat16),
+            jax.ShapeDtypeStruct((ncol, width, x_dst.shape[0]), jnp.bfloat16),
+            jax.ShapeDtypeStruct(mask.shape, jnp.bfloat16),
+        ),
+        in_specs=[vmem, vmem, hbm, hbm],
+        out_specs=(hbm, hbm, hbm),
+        scratch_shapes=[
+            pltpu.VMEM((width, x_dst.shape[0]), jnp.bfloat16),
+            pltpu.VMEM(mask.shape, jnp.int32),
+            pltpu.VMEM(mask.shape, jnp.bfloat16),
+            dma((len(sends),)),
+            dma((len(sends),)),
+            dma((ncol - 1,)),
+            dma((ncol - 1,)),
+            dma((16,)),
+            dma((16,)),
+            dma((2,)),
+        ],
+        compiler_params=pltpu.CompilerParams(
+            collective_id=0, has_side_effects=True, vmem_limit_bytes=32 * 2**20
+        ),
+        name="gather_all",
+    )(x_dst, w_query, x_src, mask)
+
+
 def attend_kernel(
-    order_ref, coords_ref, count_ref, sink_ref, x_ref, q_ref, wk_ref, wvt_ref, bias_hbm,
+    order_ref, coords_ref, count_ref, sink_ref, x_ref, q_ref, wk_ref, wv_ref, bias_hbm,
     acc_out, stat_out,
     rows, lo, hi, keys, values, qz, acc, top, total, bias, sbuf, peak, sem,
 ):
@@ -56,7 +248,7 @@
             top[d, h:h + 1, :] = jnp.full((1, tile), sink_ref[h] * math.sqrt(hd), jnp.float32)
 
     wk = wk_ref[...]
-    wvt = wvt_ref[...]
+    wvt = wv_ref[...].astype(jnp.float32).T.astype(jnp.bfloat16)
 
     def gather(b, e):
         base = b * tile
@@ -132,7 +324,7 @@
         stat_out[d, heads:, :] = total[d]
 
 
-def attend(order, coords, count, sink, x, q, wk, wvt, bias):
+def attend(order, coords, count, sink, x, q, wk, wv, bias):
     nsrc, width = x.shape
     n_dblk, _, tile = q.shape
     heads = sink.shape[0]
@@ -165,32 +357,98 @@
         ],
         compiler_params=pltpu.CompilerParams(vmem_limit_bytes=56 * 2**20),
         name="attend",
-    )(order, coords, count, sink, x, q, wk, wvt, bias)
+    )(order, coords, count, sink, x, q, wk, wv, bias)
+
+
+def finish_kernel(ncol, sink_ref, acc_ref, stat_ref, w_out, out_ref, accs, stats, a_send, a_recv, s_send, s_recv):
+    col = lax.axis_index("col")
+    heads = sink_ref.shape[0]
+    _, width, tile = acc_ref.shape
+    hd = width // heads
+
+    def peer(o):
+        return lax.rem(col + o, ncol)
+
+    barrier = pltpu.get_barrier_semaphore()
+    for o in range(1, ncol):
+        pl.semaphore_signal(barrier, inc=1, device_id={"col": peer(o)}, device_id_type=MESH)
+    pl.semaphore_wait(barrier, ncol - 1)
+
+    moves = ((stat_ref, stats, s_send, s_recv), (acc_ref, accs, a_send, a_recv))
+
+    def copy(o, which):
+        src, dst, send, recv = moves[which]
+        return pltpu.make_async_remote_copy(
+            src_ref=src.at[peer(o)],
+            dst_ref=dst.at[o - 1],
+            send_sem=send.at[o - 1],
+            recv_sem=recv.at[o - 1],
+            device_id={"col": peer(o)},
+            device_id_type=MESH,
+        )
+
+    order = sorted(range(1, ncol), key=lambda o: -min(o, ncol - o))
+    for o in order:
+        copy(o, 0).start()
+        copy(o, 1).start()
+    stat = [stat_ref[col]]
+    for o in range(1, ncol):
+        copy(o, 0).wait_recv()
+        stat.append(stats[o - 1])
+    top = functools.reduce(jnp.maximum, [s[:heads] for s in stat])
+    fades = [jnp.exp2(s[:heads] - top) for s in stat]
+    sinks = jnp.concatenate([jnp.full((1, tile), sink_ref[h] * math.log2(math.e), jnp.float32) for h in range(heads)], axis=0)
+    total = jnp.exp2(sinks - top)
+    for s, fade in zip(stat, fades):
+        total = total + s[heads:] * fade
+
+    def spread(per_head):
+        return jnp.concatenate([jnp.broadcast_to(per_head[h:h + 1], (hd, tile)) for h in range(heads)], axis=0)
+
+    mixed = acc_ref[col].astype(jnp.float32) * spread(fades[0])
+    for o in range(1, ncol):
+        copy(o, 1).wait_recv()
+        mixed = mixed + accs[o - 1].astype(jnp.float32) * spread(fades[o])
+    mixed = (mixed / spread(total)).T.astype(jnp.bfloat16)
+    out_ref[...] = jnp.dot(mixed, w_out[...], preferred_element_type=jnp.float32).astype(jnp.bfloat16)
+    for o in range(1, ncol):
+        copy(o, 0).wait_send()
+        copy(o, 1).wait_send()
+
+
+def finish(sink, acc, stat, w_out):
+    ncol, width, tile = acc.shape
+    vmem = pl.BlockSpec(memory_space=pltpu.VMEM)
+    dma = pltpu.SemaphoreType.DMA
+    return pl.pallas_call(
+        functools.partial(finish_kernel, ncol),
+        out_shape=jax.ShapeDtypeStruct((tile, width), jnp.bfloat16),
+        in_specs=[pl.BlockSpec(memory_space=pltpu.SMEM), vmem, vmem, vmem],
+        out_specs=vmem,
+        scratch_shapes=[
+            pltpu.VMEM((ncol - 1, width, tile), jnp.bfloat16),
+            pltpu.VMEM((ncol - 1,) + stat.shape[1:], jnp.float32),
+        ]
+        + [dma((ncol - 1,))] * 4,
+        compiler_params=pltpu.CompilerParams(
+            collective_id=1, has_side_effects=True, vmem_limit_bytes=16 * 2**20
+        ),
+        name="finish",
+    )(sink, acc, stat, w_out)
 
 
 def body(
-    x_dst, x_src, w_query, w_key, w_value, w_out, sink, node_order, tile_coords, tile_count, edge_mask
+    nx, nz, ncol,
+    x_dst, x_src, w_query, w_key, w_value, w_out, sink, node_order, tile_coords, tile_count, edge_mask,
 ):
-    heads = sink.shape[0]
-    width = x_dst.shape[1]
-    hd = width // heads
-    tile = edge_mask.shape[-1]
-    x = lax.all_gather(x_src[0], "row", axis=0, tiled=True)
-    q_own = dot_nt(w_query.T, x_dst).astype(jnp.bfloat16)
-    q = lax.all_gather(q_own, "col", axis=0)
-    bias = jnp.where(edge_mask[0, 0] == 1, 0.0, MASKED).astype(jnp.bfloat16).swapaxes(1, 2)
+    x, q, bias = gather_all(nx, nz, ncol, x_dst, w_query, x_src[0], edge_mask[0, 0])
     acc, stat = attend(
-        node_order[0], tile_coords[0, 0], tile_count[0], sink, x, q, w_key, w_value.T, bias
+        node_order[0], tile_coords[0, 0], tile_count[0], sink, x.reshape(-1, x.shape[-1]), q, w_key, w_value, bias
     )
-    acc = lax.all_to_all(acc, "col", 0, 0).astype(jnp.float32)
-    stat = lax.all_to_all(stat, "col", 0, 0)
-    tops, totals = stat[:, :heads], stat[:, heads:]
-    top = jnp.max(tops, axis=0)
-    fade = jnp.exp2(tops - top)
-    denom = jnp.sum(totals * fade, axis=0) + jnp.exp2(sink[:, None] * math.log2(math.e) - top)
-    acc = jnp.sum(acc.reshape(-1, heads, hd, tile) * fade[:, :, None, :], axis=0)
-    mixed = (acc / denom[:, None, :]).reshape(width, tile).T.astype(jnp.bfloat16)
-    return jnp.dot(mixed, w_out, preferred_element_type=jnp.float32).astype(jnp.bfloat16)
+    return finish(sink, acc, stat, w_out)
+
+
+NX = 4
 
 
 def solution(mesh):
@@ -208,4 +466,6 @@
         P("row", "col", None, None, None),
     )
     out_specs = P(("row", "col"), None)
-    return jax.shard_map(body, mesh=mesh, in_specs=in_specs, out_specs=out_specs, check_vma=False)
+    nrow, ncol = mesh.shape["row"], mesh.shape["col"]
+    program = functools.partial(body, NX, nrow // NX, ncol)
+    return jax.shard_map(program, mesh=mesh, in_specs=in_specs, out_specs=out_specs, check_vma=False)

time: 170 us -> 109 us (0.64)
  the two profiles are of different devices: /device:TPU:4 before, /device:TPU:1 now
where the time goes in v2:
time: 109 us
  Pallas kernels  94.9 us (87%)
  local copies, waits for them, and re-layouts  13.3 us (12%)
    pallas_call x1, Pallas kernels, gather_all(): pl.pallas_call(functools.partial(gather_kernel, nx, nz, ncol, sends, even...  37 us
    pallas_call x1, Pallas kernels, attend(): pl.pallas_call(attend_kernel, out_shape=(jax.ShapeDtypeStruct((n_dblk, wi...  29.3 us
    pallas_call x1, Pallas kernels, finish(): pl.pallas_call(functools.partial(finish_kernel, ncol), out_shape=jax.Shap...  28.6 us
    unnamed x23, local copies, waits for them, and re-layouts  13.3 us

profile of v2, /device:TPU:1, one launch (start us, length us, event | category | flops | bytes accessed | tf_op | source)
XLA Modules:
  0.0 108.8 jit_solution(11883452904209384531)
XLA Ops:
  0.7 0.0 copy-start
  0.7 3.4 %copy-done = s32[1,1,128,128,128]{4,3,2,1,0:T(8,128)S(1)} copy-done((s32[1,1,128,128,128]{4,3,2,1,0:T(8,128)S(1)}, s32[1,1,128,128,128]{4,3,2,1,0:T(8,128)}, u32[]{:S(2)}) %copy-start) | copy-done | bytes 8388632
  4.0 0.9 copy-done.5
  4.9 0.0 copy-start.6
  4.9 0.9 copy-done.6
  5.8 0.0 copy-start.8
  5.8 0.8 copy-done.8
  6.7 37.0 %gather_all.1 = (bf16[32,256,256]{2,1,0:T(8,128)(2,1)S(1)}, bf16[8,256,128]{2,1,0:T(8,128)(2,1)S(1)}, bf16[128,128,128]{2,1,0:T(8,128)(2,1)S(1)}) custom-call(bf16[128,256]{1,0:T(8,128)(2,1)S(1)} %copy-done.8, bf16[256,256]{1,0:T(8,128)(2,1)S(1)} %copy-done.5, bf16[256,256]{1,0:T(8,128)(2,1)S(1)} %bitcast.9, s32[128,128,128]{2,1,0:T(8,128)S(1)} %bitcast.7), custom_call_target="tpu_custom_call" | custom-call | tf_op jit(solution)/shard_map/gather_all/pallas_call | solution.py:184
  43.7 0.0 copy-start.1
  43.7 1.9 %copy-done.1 = bf16[32,256,256]{2,1,0:T(8,128)(2,1)} copy-done((bf16[32,256,256]{2,1,0:T(8,128)(2,1)}, bf16[32,256,256]{2,1,0:T(8,128)(2,1)S(1)}, u32[]{:S(2)}) %copy-start.1) | copy-done | bytes 4194328
  45.7 0.0 copy-start.2
  45.7 2.0 %copy-done.2 = bf16[128,128,128]{2,1,0:T(8,128)(2,1)} copy-done((bf16[128,128,128]{2,1,0:T(8,128)(2,1)}, bf16[128,128,128]{2,1,0:T(8,128)(2,1)S(1)}, u32[]{:S(2)}) %copy-start.2) | copy-done | bytes 4194328
  47.6 0.0 copy-start.3
  47.6 0.8 copy-done.3
  48.5 0.0 copy-start.7
  48.5 0.0 copy-start.10
  48.5 29.3 %attend.1 = (bf16[8,256,128]{2,1,0:T(8,128)(2,1)}, f32[8,16,128]{2,1,0:T(8,128)}) custom-call(s32[8192]{0:T(1024)} %bitcast.10, s32[2,128]{1,0:T(2,128)} %bitcast.11, s32[1]{0:T(128)} %bitcast.6.count_ref, f32[8]{0:T(128)} %sink_ref.3, bf16[8192,256]{1,0:T(8,128)(2,1)} %bitcast.8, bf16[8,256,128]{2,1,0:T(8,128)(2,1)} %copy-done.3, bf16[256,256]{1,0:T(8,128)(2,1)} %wk_ref.1, ...), custom_call_target="tpu_custom_call" | custom-call | tf_op jit(solution)/shard_map/attend/pallas_call | solution.py:335
  77.7 0.0 copy-done.7
  77.7 0.0 copy-done.10
  77.8 0.0 copy-start.4
  77.8 1.0 copy-done.4
  78.8 0.8 copy-done.9
  79.6 28.6 %finish.1 = bf16[128,256]{1,0:T(8,128)(2,1)S(1)} custom-call(f32[8]{0:T(128)S(1)} %copy-done.10, bf16[8,256,128]{2,1,0:T(8,128)(2,1)S(1)} %copy-done.4, f32[8,16,128]{2,1,0:T(8,128)S(1)} %copy-done.9, bf16[256,256]{1,0:T(8,128)(2,1)S(1)} %copy-done.7), custom_call_target="tpu_custom_call" | custom-call | tf_op jit(solution)/shard_map/finish/pallas_call | solution.py:423
  108.2 0.6 copy.14
  (2 shorter events, 0.0 us)
Async XLA Ops:
  0.7 3.4 %copy-start = (s32[1,1,128,128,128]{4,3,2,1,0:T(8,128)S(1)}, s32[1,1,128,128,128]{4,3,2,1,0:T(8,128)}, u32[]{:S(2)}) copy-start(s32[1,1,128,128,128]{4,3,2,1,0:T(8,128)} %param.21) | copy-start | bytes 25165828
  4.0 0.9 copy-start.5
  4.9 0.9 copy-start.6
  5.8 0.8 copy-start.8
  43.7 2.0 %copy-start.1 = (bf16[32,256,256]{2,1,0:T(8,128)(2,1)}, bf16[32,256,256]{2,1,0:T(8,128)(2,1)S(1)}, u32[]{:S(2)}) copy-start(bf16[32,256,256]{2,1,0:T(8,128)(2,1)S(1)} %get-tuple-element.10) | copy-start | bytes 12582916
  45.7 2.0 %copy-start.2 = (bf16[128,128,128]{2,1,0:T(8,128)(2,1)}, bf16[128,128,128]{2,1,0:T(8,128)(2,1)S(1)}, u32[]{:S(2)}) copy-start(bf16[128,128,128]{2,1,0:T(8,128)(2,1)S(1)} %get-tuple-element.12.bias_hbm) | copy-start | bytes 12582916
  47.6 0.8 copy-start.3
  48.5 29.3 %copy-start.7 = (bf16[256,256]{1,0:T(8,128)(2,1)S(1)}, bf16[256,256]{1,0:T(8,128)(2,1)}, u32[]{:S(2)}) copy-start(bf16[256,256]{1,0:T(8,128)(2,1)} %w_out.1) | copy-start | bytes 393220
  48.5 29.3 %copy-start.10 = (f32[8]{0:T(128)S(1)}, f32[8]{0:T(128)}, u32[]{:S(2)}) copy-start(f32[8]{0:T(128)} %sink_ref.3) | copy-start | bytes 100
  77.8 1.0 copy-start.4
  78.8 0.8 copy-start.9

commit v3 on v2

--- a/solution.py
+++ b/solution.py
@@ -9,8 +9,9 @@
 from jax.sharding import PartitionSpec as P
 
 MASKED = -1e30
-UNROLL = 8
-TILE = 128
+UNROLL = 16
+BATCH = 8
+CHUNKS = 8
 
 
 def dot_nt(a, b):
@@ -68,9 +69,9 @@
 
 def gather_kernel(
     nx, nz, ncol, sends, events,
-    x_dst, w_query, x_src, mask_hbm,
+    x_dst_hbm, w_query_hbm, x_src, mask_hbm,
     x_all, q_all, bias_hbm,
-    q_own, masks, bias, send_sem, recv_sem, q_send, q_recv, in_sem, out_sem, own_sem,
+    x_dst, w_query, q_own, masks, bias, send_sem, recv_sem, q_send, q_recv, in_sem, out_sem, own_sem,
 ):
     row, col = lax.axis_index("row"), lax.axis_index("col")
     z, x = row // nx, lax.rem(row, nx)
@@ -97,6 +98,12 @@
         pl.semaphore_signal(barrier, inc=1, device_id={"row": at(*STEP[link])}, device_id_type=MESH)
     for o in range(1, ncol):
         pl.semaphore_signal(barrier, inc=1, device_id={"col": peer(o)}, device_id_type=MESH)
+    operands = [
+        pltpu.make_async_copy(x_dst_hbm, x_dst, own_sem.at[2]),
+        pltpu.make_async_copy(w_query_hbm, w_query, own_sem.at[3]),
+    ]
+    for copy in operands:
+        copy.start()
     for i in range(chunks):
         loaded(i).start()
     own_x = pltpu.make_async_copy(x_src, x_all.at[row], own_sem.at[0])
@@ -151,6 +158,8 @@
             piece(k, False).start()
         else:
             if own_q is None:
+                for copy in operands:
+                    copy.wait()
                 q = jnp.dot(x_dst[...], w_query[...], preferred_element_type=jnp.float32)
                 q_own[...] = q.T.astype(jnp.bfloat16)
                 for o in range(1, ncol):
@@ -178,8 +187,7 @@
     rows, width = x_src.shape
     slots, tile, _ = mask.shape
     sends, events = spread_plan(nx, nz, rows)
-    vmem = pl.BlockSpec(memory_space=pltpu.VMEM)
-    hbm = pl.BlockSpec(memory_space=pl.ANY)
+    hbm = pl.BlockSpec(memory_space=pltpu.HBM)
     dma = pltpu.SemaphoreType.DMA
     return pl.pallas_call(
         functools.partial(gather_kernel, nx, nz, ncol, sends, events),
@@ -188,9 +196,11 @@
             jax.ShapeDtypeStruct((ncol, width, x_dst.shape[0]), jnp.bfloat16),
             jax.ShapeDtypeStruct(mask.shape, jnp.bfloat16),
         ),
-        in_specs=[vmem, vmem, hbm, hbm],
+        in_specs=[hbm, hbm, hbm, hbm],
         out_specs=(hbm, hbm, hbm),
         scratch_shapes=[
+            pltpu.VMEM(x_dst.shape, jnp.bfloat16),
+            pltpu.VMEM(w_query.shape, jnp.bfloat16),
             pltpu.VMEM((width, x_dst.shape[0]), jnp.bfloat16),
             pltpu.VMEM(mask.shape, jnp.int32),
             pltpu.VMEM(mask.shape, jnp.bfloat16),
@@ -200,41 +210,58 @@
             dma((ncol - 1,)),
             dma((16,)),
             dma((16,)),
-            dma((2,)),
+            dma((4,)),
         ],
         compiler_params=pltpu.CompilerParams(
-            collective_id=0, has_side_effects=True, vmem_limit_bytes=32 * 2**20
+            collective_id=0, has_side_effects=True, vmem_limit_bytes=58 * 2**20
         ),
         name="gather_all",
     )(x_dst, w_query, x_src, mask)
 
 
 def attend_kernel(
-    order_ref, coords_ref, count_ref, sink_ref, x_ref, q_ref, wk_ref, wv_ref, bias_hbm,
+    coords_ref, count_ref, sink_ref, order_hbm, x_hbm, q_hbm, wk_hbm, wv_hbm, bias_hbm,
     acc_out, stat_out,
-    rows, lo, hi, keys, values, qz, acc, top, total, bias, sbuf, peak, sem,
+    order_ref, x_ref, q_ref, wk_ref, wv_ref, rows, picked, keys, values, qz, acc, top, total, bias, sbuf, peak,
+    x_sem, sem,
 ):
     heads = sink_ref.shape[0]
-    n_dblk, width, tile = q_ref.shape
+    n_dblk, width, tile = q_hbm.shape
     hd = width // heads
     half = width // 2
     per_half = heads // 2
     c = math.log2(math.e) / math.sqrt(hd)
-    nsrc = x_ref.shape[0]
+    nsrc = x_hbm.shape[0]
     nblk = nsrc // tile
     slots = bias_hbm.shape[0]
-    count = count_ref[0]
-    load = pltpu.make_async_copy(bias_hbm, bias.at[pl.ds(0, slots)], sem.at[0])
-    load.start()
-
-    @pl.loop(0, nsrc // 256)
-    def _(i):
-        r = pl.ds(pl.multiple_of(i * 256, 256), 256)
-        v = x_ref[r, :].astype(jnp.float32)
-        rows[0, r, :] = v[:, :half]
-        rows[1, r, :] = v[:, half:]
+    count = count_ref[0, 0]
+    part = nsrc // CHUNKS
+
+    def x_load(i):
+        r = pl.ds(i * part, part)
+        return pltpu.make_async_copy(x_hbm.at[r], x_ref.at[r], x_sem.at[i])
+
+    loads = [
+        pltpu.make_async_copy(src, dst, sem.at[i])
+        for i, (src, dst) in enumerate(
+            (
+                (q_hbm, q_ref),
+                (order_hbm, order_ref),
+                (wk_hbm, wk_ref),
+                (wv_hbm, wv_ref),
+                (bias_hbm, bias.at[pl.ds(0, slots)]),
+            )
+        )
+    ]
+    for load in loads[:1]:
+        load.start()
+    for i in range(CHUNKS):
+        x_load(i).start()
+    for load in loads[1:]:
+        load.start()
 
     qz[...] = jnp.zeros_like(qz)
+    loads[0].wait()
     for d in range(n_dblk):
         for h in range(heads):
             hh = h % per_half
@@ -247,31 +274,37 @@
         for h in range(heads):
             top[d, h:h + 1, :] = jnp.full((1, tile), sink_ref[h] * math.sqrt(hd), jnp.float32)
 
+    for i in range(CHUNKS):
+        x_load(i).wait()
+
+        @pl.loop(0, part // 256)
+        def _(j):
+            first = pl.multiple_of(i * part + j * 256, 256)
+            v = x_ref[pl.ds(first, 256), :].astype(jnp.float32)
+            rows[pl.ds(2 * first, 256, stride=2), :] = v[:, :half]
+            rows[pl.ds(2 * first + 1, 256, stride=2), :] = v[:, half:]
+
+    for load in loads[1:4]:
+        load.wait()
     wk = wk_ref[...]
     wvt = wv_ref[...].astype(jnp.float32).T.astype(jnp.bfloat16)
-
-    def gather(b, e):
-        base = b * tile
-        for r in range(tile):
-            idx = order_ref[base + r]
-            lo[e, r:r + 1, :] = rows[0, pl.ds(idx, 1), :]
-            hi[e, r:r + 1, :] = rows[1, pl.ds(idx, 1), :]
-
-    def project(b, e):
-        x = jnp.concatenate([lo[e].astype(jnp.bfloat16), hi[e].astype(jnp.bfloat16)], axis=1)
-        keys[b] = jnp.dot(x, wk, preferred_element_type=jnp.float32).astype(jnp.bfloat16)
-        values[b] = dot_nt(wvt, x).astype(jnp.bfloat16)
-
-    gather(0, 0)
-
-    @pl.loop(0, nblk // 2)
+    batch = BATCH * tile
+
+    @pl.loop(0, nblk // BATCH)
     def _(i):
-        gather(2 * i + 1, 1)
-        project(2 * i, 0)
-        gather(jnp.minimum(2 * i + 2, nblk - 1), 0)
-        project(2 * i + 1, 1)
-
-    load.wait()
+        for r in range(batch):
+            idx = order_ref[i * batch + r]
+            picked[2 * r:2 * r + 2, :] = rows[pl.ds(pl.multiple_of(2 * idx, 2), 2), :]
+        lo = picked[pl.ds(0, batch, stride=2), :].astype(jnp.bfloat16)
+        hi = picked[pl.ds(1, batch, stride=2), :].astype(jnp.bfloat16)
+        x = jnp.concatenate([lo, hi], axis=1)
+        k = jnp.dot(x, wk, preferred_element_type=jnp.float32).astype(jnp.bfloat16)
+        v = dot_nt(wvt, x).astype(jnp.bfloat16)
+        for j in range(BATCH):
+            keys[i * BATCH + j] = k[j * tile:(j + 1) * tile]
+            values[i * BATCH + j] = v[:, j * tile:(j + 1) * tile]
+
+    loads[4].wait()
     ones = jnp.ones((16, tile), jnp.bfloat16)
 
     def place(t):
@@ -332,18 +365,23 @@
     nblk = nsrc // tile
     smem = pl.BlockSpec(memory_space=pltpu.SMEM)
     vmem = pl.BlockSpec(memory_space=pltpu.VMEM)
+    hbm = pl.BlockSpec(memory_space=pltpu.HBM)
     return pl.pallas_call(
         attend_kernel,
         out_shape=(
             jax.ShapeDtypeStruct((n_dblk, width, tile), jnp.bfloat16),
             jax.ShapeDtypeStruct((n_dblk, 2 * heads, tile), jnp.float32),
         ),
-        in_specs=[smem] * 4 + [vmem] * 4 + [pl.BlockSpec(memory_space=pl.ANY)],
+        in_specs=[smem] * 3 + [hbm] * 6,
         out_specs=(vmem, vmem),
         scratch_shapes=[
-            pltpu.VMEM((2, nsrc, width // 2), jnp.float32),
-            pltpu.VMEM((2, tile, width // 2), jnp.float32),
-            pltpu.VMEM((2, tile, width // 2), jnp.float32),
+            pltpu.SMEM((nsrc,), jnp.int32),
+            pltpu.VMEM((nsrc, width), jnp.bfloat16),
+            pltpu.VMEM(q.shape, jnp.bfloat16),
+            pltpu.VMEM((width, width), jnp.bfloat16),
+            pltpu.VMEM((width, width), jnp.bfloat16),
+            pltpu.VMEM((2 * nsrc, width // 2), jnp.float32),
+            pltpu.VMEM((2 * BATCH * tile, width // 2), jnp.float32),
             pltpu.VMEM((nblk, tile, width), jnp.bfloat16),
             pltpu.VMEM((nblk, width, tile), jnp.bfloat16),
             pltpu.VMEM((n_dblk, width // 2, heads * tile), jnp.bfloat16),
@@ -353,14 +391,20 @@
             pltpu.VMEM((slots + 1, tile, tile), jnp.bfloat16),
             pltpu.VMEM((2, heads, tile, tile), jnp.float32),
             pltpu.VMEM((2, heads, tile), jnp.float32),
-            pltpu.SemaphoreType.DMA((1,)),
+            pltpu.SemaphoreType.DMA((CHUNKS,)),
+            pltpu.SemaphoreType.DMA((5,)),
         ],
-        compiler_params=pltpu.CompilerParams(vmem_limit_bytes=56 * 2**20),
+        compiler_params=pltpu.CompilerParams(vmem_limit_bytes=58 * 2**20),
         name="attend",
-    )(order, coords, count, sink, x, q, wk, wv, bias)
-
-
-def finish_kernel(ncol, sink_ref, acc_ref, stat_ref, w_out, out_ref, accs, stats, a_send, a_recv, s_send, s_recv):
+    )(coords, count, sink, order, x, q, wk, wv, bias)
+
+
+def finish_kernel(
+    ncol,
+    sink_ref, acc_ref, stat_ref, w_out_hbm,
+    out_ref,
+    accs, stats, acc_own, stat_own, w_out, a_send, a_recv, s_send, s_recv, own_sem,
+):
     col = lax.axis_index("col")
     heads = sink_ref.shape[0]
     _, width, tile = acc_ref.shape
@@ -372,6 +416,13 @@
     barrier = pltpu.get_barrier_semaphore()
     for o in range(1, ncol):
         pl.semaphore_signal(barrier, inc=1, device_id={"col": peer(o)}, device_id_type=MESH)
+    own = [
+        pltpu.make_async_copy(stat_ref.at[col], stat_own, own_sem.at[0]),
+        pltpu.make_async_copy(acc_ref.at[col], acc_own, own_sem.at[1]),
+        pltpu.make_async_copy(w_out_hbm, w_out, own_sem.at[2]),
+    ]
+    for load in own:
+        load.start()
     pl.semaphore_wait(barrier, ncol - 1)
 
     moves = ((stat_ref, stats, s_send, s_recv), (acc_ref, accs, a_send, a_recv))
@@ -391,7 +442,9 @@
     for o in order:
         copy(o, 0).start()
         copy(o, 1).start()
-    stat = [stat_ref[col]]
+    for load in own:
+        load.wait()
+    stat = [stat_own[...]]
     for o in range(1, ncol):
         copy(o, 0).wait_recv()
         stat.append(stats[o - 1])
@@ -405,7 +458,7 @@
     def spread(per_head):
         return jnp.concatenate([jnp.broadcast_to(per_head[h:h + 1], (hd, tile)) for h in range(heads)], axis=0)
 
-    mixed = acc_ref[col].astype(jnp.float32) * spread(fades[0])
+    mixed = acc_own[...].astype(jnp.float32) * spread(fades[0])
     for o in range(1, ncol):
         copy(o, 1).wait_recv()
         mixed = mixed + accs[o - 1].astype(jnp.float32) * spread(fades[o])
@@ -418,20 +471,24 @@
 
 def finish(sink, acc, stat, w_out):
     ncol, width, tile = acc.shape
-    vmem = pl.BlockSpec(memory_space=pltpu.VMEM)
+    hbm = pl.BlockSpec(memory_space=pltpu.HBM)
     dma = pltpu.SemaphoreType.DMA
     return pl.pallas_call(
         functools.partial(finish_kernel, ncol),
         out_shape=jax.ShapeDtypeStruct((tile, width), jnp.bfloat16),
-        in_specs=[pl.BlockSpec(memory_space=pltpu.SMEM), vmem, vmem, vmem],
-        out_specs=vmem,
+        in_specs=[pl.BlockSpec(memory_space=pltpu.SMEM), hbm, hbm, hbm],
+        out_specs=pl.BlockSpec(memory_space=pltpu.VMEM),
         scratch_shapes=[
             pltpu.VMEM((ncol - 1, width, tile), jnp.bfloat16),
             pltpu.VMEM((ncol - 1,) + stat.shape[1:], jnp.float32),
+            pltpu.VMEM((width, tile), jnp.bfloat16),
+            pltpu.VMEM(stat.shape[1:], jnp.float32),
+            pltpu.VMEM(w_out.shape, jnp.bfloat16),
         ]
-        + [dma((ncol - 1,))] * 4,
+        + [dma((ncol - 1,))] * 4
+        + [dma((3,))],
         compiler_params=pltpu.CompilerParams(
-            collective_id=1, has_side_effects=True, vmem_limit_bytes=16 * 2**20
+            collective_id=1, has_side_effects=True, vmem_limit_bytes=58 * 2**20
         ),
         name="finish",
     )(sink, acc, stat, w_out)
@@ -443,7 +500,7 @@
 ):
     x, q, bias = gather_all(nx, nz, ncol, x_dst, w_query, x_src[0], edge_mask[0, 0])
     acc, stat = attend(
-        node_order[0], tile_coords[0, 0], tile_count[0], sink, x.reshape(-1, x.shape[-1]), q, w_key, w_value, bias
+        node_order[0], tile_coords[0, 0], tile_count, sink, x.reshape(-1, x.shape[-1]), q, w_key, w_value, bias
     )
     return finish(sink, acc, stat, w_out)
 

time: 109 us -> 93.9 us (0.86)
  the two profiles are of different devices: /device:TPU:1 before, /device:TPU:4 now
where the time goes in v3:
time: 93.9 us; the launch traced here: 93.8 us
  Pallas kernels  91.6 us (98%)
  local copies, waits for them, and re-layouts  1.47 us (2%)
    pallas_call x1, Pallas kernels, gather_all(): pl.pallas_call(functools.partial(gather_kernel, nx, nz, ncol, sends, even...  41.9 us
    pallas_call x1, Pallas kernels, attend(): pl.pallas_call(attend_kernel, out_shape=(jax.ShapeDtypeStruct((n_dblk, wi...  36.8 us
    pallas_call x1, Pallas kernels, finish(): pl.pallas_call(functools.partial(finish_kernel, ncol), out_shape=jax.Shap...  12.9 us

profile of v3, /device:TPU:4, one launch (start us, length us, event | category | flops | bytes accessed | tf_op | source)
XLA Modules:
  0.0 93.8 jit_solution(7753642525058647276)
XLA Ops:
  0.7 41.9 %gather_all.1 = (bf16[32,256,256]{2,1,0:T(8,128)(2,1)}, bf16[8,256,128]{2,1,0:T(8,128)(2,1)}, bf16[128,128,128]{2,1,0:T(8,128)(2,1)}) custom-call(bf16[128,256]{1,0:T(8,128)(2,1)} %x_dst_hbm.1, bf16[256,256]{1,0:T(8,128)(2,1)} %w_query_hbm.1, bf16[256,256]{1,0:T(8,128)(2,1)} %bitcast.7, s32[128,128,128]{2,1,0:T(8,128)} %bitcast.5), custom_call_target="tpu_custom_call" | custom-call | tf_op jit(solution)/shard_map/gather_all/pallas_call | solution.py:192
  42.6 36.8 %attend.1 = (bf16[8,256,128]{2,1,0:T(8,128)(2,1)}, f32[8,16,128]{2,1,0:T(8,128)}) custom-call(s32[2,128]{1,0:T(2,128)} %bitcast.9, s32[1,1]{1,0:T(1,128)S(6)} %copy.13.count_ref, f32[8]{0:T(128)} %sink_ref.3, s32[8192]{0:T(1024)} %bitcast.8, bf16[8192,256]{1,0:T(8,128)(2,1)} %bitcast.6, bf16[8,256,128]{2,1,0:T(8,128)(2,1)} %get-tuple-element.11.q_hbm, ...), custom_call_target="tpu_custom_call" | custom-call | tf_op jit(solution)/shard_map/attend/pallas_call | solution.py:369
  79.3 12.9 %finish.1 = bf16[128,256]{1,0:T(8,128)(2,1)} custom-call(f32[8]{0:T(128)} %sink_ref.3, bf16[8,256,128]{2,1,0:T(8,128)(2,1)} %get-tuple-element.13.acc_ref, f32[8,16,128]{2,1,0:T(8,128)} %get-tuple-element.14.stat_ref, bf16[256,256]{1,0:T(8,128)(2,1)} %w_out_hbm.1), custom_call_target="tpu_custom_call" | custom-call | tf_op jit(solution)/shard_map/finish/pallas_call | solution.py:476
  92.3 1.5 %copy.14 = bf16[128,256]{1,0:T(8,128)(2,1)} copy(bf16[128,256]{1,0:T(8,128)(2,1)} %finish.1) | data formatting | bytes 131072

commit v4 on v3

--- a/solution.py
+++ b/solution.py
@@ -9,7 +9,7 @@
 from jax.sharding import PartitionSpec as P
 
 MASKED = -1e30
-UNROLL = 16
+UNROLL = 32
 BATCH = 8
 CHUNKS = 8
 
@@ -311,45 +311,49 @@
         u = jnp.minimum(t, slots - 1)
         return coords_ref[0, u], coords_ref[1, u]
 
-    def scores(t, e):
+    def scores(e, hp, d, b, bt):
+        g = 2 * hp // per_half
+        pair = jnp.dot(
+            keys[b, :, g * half:(g + 1) * half],
+            qz[d, :, 2 * hp * tile:2 * (hp + 1) * tile],
+            preferred_element_type=jnp.float32,
+        )
+        for i in range(2):
+            s = pair[:, i * tile:(i + 1) * tile] + bt
+            sbuf[e, 2 * hp + i] = s
+            peak[e, 2 * hp + i:2 * hp + i + 1, :] = jnp.max(s, axis=0, keepdims=True)
+
+    def terms(t):
+        return bias[jnp.where(t < count, t, slots)].astype(jnp.float32)
+
+    def step(t, e):
         d, b = place(t)
-        bt = bias[jnp.where(t < count, t, slots)].astype(jnp.float32)
-        for hp in range(heads // 2):
-            g = 2 * hp // per_half
-            pair = jnp.dot(
-                keys[b, :, g * half:(g + 1) * half],
-                qz[d, :, 2 * hp * tile:2 * (hp + 1) * tile],
-                preferred_element_type=jnp.float32,
-            )
-            for i in range(2):
-                s = pair[:, i * tile:(i + 1) * tile] + bt
-                sbuf[e, 2 * hp + i] = s
-                peak[e, 2 * hp + i:2 * hp + i + 1, :] = jnp.max(s, axis=0, keepdims=True)
-
-    def weigh(t, e):
-        d, b = place(t)
+        dn, bn = place(t + 1)
+        bt = terms(t + 1)
         before = top[d]
         now = jnp.maximum(before, peak[e])
         fade = jnp.exp2((before - now) * c)
         top[d] = now
         sums = []
-        for h in range(heads):
-            f = slice(h * hd, (h + 1) * hd)
-            p = jnp.exp2((sbuf[e, h] - now[h:h + 1]) * c).astype(jnp.bfloat16)
-            v = jnp.concatenate([values[b, f, :], ones], axis=0)
-            o = jnp.dot(v, p, preferred_element_type=jnp.float32)
-            acc[d, f, :] = acc[d, f, :] * fade[h:h + 1] + o[:hd]
-            sums.append(o[hd:hd + 1])
+        for hp in range(heads // 2):
+            scores(1 - e, hp, dn, bn, bt)
+            for h in (2 * hp, 2 * hp + 1):
+                f = slice(h * hd, (h + 1) * hd)
+                p = jnp.exp2((sbuf[e, h] - now[h:h + 1]) * c).astype(jnp.bfloat16)
+                v = jnp.concatenate([values[b, f, :], ones], axis=0)
+                o = jnp.dot(v, p, preferred_element_type=jnp.float32)
+                acc[d, f, :] = acc[d, f, :] * fade[h:h + 1] + o[:hd]
+                sums.append(o[hd:hd + 1])
         total[d] = total[d] * fade + jnp.concatenate(sums, axis=0)
 
-    scores(0, 0)
+    d0, b0 = place(0)
+    for hp in range(heads // 2):
+        scores(0, hp, d0, b0, terms(0))
 
     @pl.loop(0, (count + UNROLL - 1) // UNROLL)
     def _(i):
         for u in range(UNROLL):
-            t = i * UNROLL + u
-            scores(t + 1, (u + 1) % 2)
-            weigh(t, u % 2)
+            step(i * UNROLL + u, u % 2)
 
     acc_out[...] = acc[...].astype(jnp.bfloat16)
     for d in range(n_dblk):

time: 93.9 us -> 91.4 us (0.973)
  Pallas kernels: 91.6 us -> 89.1 us
    pallas_call x1, Pallas kernels: 36.8 us -> 34.2 us  [attend(): pl.pallas_call(attend_kernel, out_shape=(jax.ShapeDtypeStruct((n_dblk, wi...]
where the time goes in v4:
time: 91.4 us; the launch traced here: 91.3 us
  Pallas kernels  89.1 us (97%)
  local copies, waits for them, and re-layouts  1.47 us (2%)
    pallas_call x1, Pallas kernels, gather_all(): pl.pallas_call(functools.partial(gather_kernel, nx, nz, ncol, sends, even...  41.9 us
    pallas_call x1, Pallas kernels, attend(): pl.pallas_call(attend_kernel, out_shape=(jax.ShapeDtypeStruct((n_dblk, wi...  34.2 us
    pallas_call x1, Pallas kernels, finish(): pl.pallas_call(functools.partial(finish_kernel, ncol), out_shape=jax.Shap...  13 us

profile of v4, /device:TPU:4, one launch (start us, length us, event | category | flops | bytes accessed | tf_op | source)
XLA Modules:
  0.0 91.3 jit_solution(13665400237594124918)
XLA Ops:
  0.7 41.9 %gather_all.1 = (bf16[32,256,256]{2,1,0:T(8,128)(2,1)}, bf16[8,256,128]{2,1,0:T(8,128)(2,1)}, bf16[128,128,128]{2,1,0:T(8,128)(2,1)}) custom-call(bf16[128,256]{1,0:T(8,128)(2,1)} %x_dst_hbm.1, bf16[256,256]{1,0:T(8,128)(2,1)} %w_query_hbm.1, bf16[256,256]{1,0:T(8,128)(2,1)} %bitcast.7, s32[128,128,128]{2,1,0:T(8,128)} %bitcast.5), custom_call_target="tpu_custom_call" | custom-call | tf_op jit(solution)/shard_map/gather_all/pallas_call | solution.py:192
  42.6 34.2 %attend.1 = (bf16[8,256,128]{2,1,0:T(8,128)(2,1)}, f32[8,16,128]{2,1,0:T(8,128)}) custom-call(s32[2,128]{1,0:T(2,128)} %bitcast.9, s32[1,1]{1,0:T(1,128)S(6)} %copy.13.count_ref, f32[8]{0:T(128)} %sink_ref.3, s32[8192]{0:T(1024)} %bitcast.8, bf16[8192,256]{1,0:T(8,128)(2,1)} %bitcast.6, bf16[8,256,128]{2,1,0:T(8,128)(2,1)} %get-tuple-element.11.q_hbm, ...), custom_call_target="tpu_custom_call" | custom-call | tf_op jit(solution)/shard_map/attend/pallas_call | solution.py:373
  76.8 13.0 %finish.1 = bf16[128,256]{1,0:T(8,128)(2,1)} custom-call(f32[8]{0:T(128)} %sink_ref.3, bf16[8,256,128]{2,1,0:T(8,128)(2,1)} %get-tuple-element.13.acc_ref, f32[8,16,128]{2,1,0:T(8,128)} %get-tuple-element.14.stat_ref, bf16[256,256]{1,0:T(8,128)(2,1)} %w_out_hbm.1), custom_call_target="tpu_custom_call" | custom-call | tf_op jit(solution)/shard_map/finish/pallas_call | solution.py:480
  89.8 1.5 %copy.14 = bf16[128,256]{1,0:T(8,128)(2,1)} copy(bf16[128,256]{1,0:T(8,128)(2,1)} %finish.1) | data formatting | bytes 131072
